TPU v7x, 32 devices: a whole 2x2x4 slice. The times are simulated.
32 devices in a mesh: day: 8 (over z, core), row: 2 (over y), col: 2 (over x).
Axes of the slice: x: 2, y: 2, z: 4, core: 2. Of those that a mesh axis runs over, the one named last changes fastest.
Arguments:
- traces: bfloat16 [896, 128, 256], P('day', ('col', 'row')), may hold values from -64 to 64
- valid: int32 [896, 128], P('day', ('col', 'row')), may hold values 0 or 1
Outputs:
- cross: float32 [2, 32, 2, 64, 128], P(None, 'day', None, 'row', 'col')
All inputs are finite; a program needn't handle non-finite values. No bound on the sum of `valid` on one device may be relied on, other than what follows from the above.
Results may differ from a plain program's by a relative error of at most 0.0025.
Values may be sent and summed in bfloat16 or wider, within the bound.
No kernel may reach another device: no remote copies, remote signals or barrier semaphores. Data moves between devices by JAX's collectives and lax.ppermute only.
A program may use at most 64 MiB of HBM per device.

v0:
```python
import math

import jax
import jax.numpy as jnp
from jax import lax
from jax.sharding import PartitionSpec as P

L = 256
F = 32
K0 = 16


def dft_table(length, nbins, first_bin):
    sample = jnp.arange(length, dtype=jnp.int32)
    bins = first_bin + jnp.arange(nbins, dtype=jnp.int32)
    angle = (sample[:, None] * bins[None, :] % length).astype(jnp.float32) * (
        2.0 * math.pi / length
    )
    taper = 0.5 - 0.5 * jnp.cos((sample.astype(jnp.float32) + 0.5) * (2.0 * math.pi / length))
    table = jnp.concatenate(
        [taper[:, None] * jnp.cos(angle), -taper[:, None] * jnp.sin(angle)], axis=1
    )
    return table.astype(jnp.bfloat16)


def pair_maker(receiver_spectra, source_part):
    nbins, doubled, width = source_part.shape
    halves = source_part.reshape(nbins, 2, doubled // 2, width)
    turned = jnp.concatenate([halves[:, 1], -halves[:, 0]], axis=1)
    real_part = jnp.einsum(
        "fwi,fwj->fij", source_part, receiver_spectra, preferred_element_type=jnp.float32
    )
    imag_part = jnp.einsum(
        "fwi,fwj->fij", turned, receiver_spectra, preferred_element_type=jnp.float32
    )
    return jnp.stack([real_part, imag_part])


def shards(traces, valid):
    windows_here, channels_here, length = traces.shape
    spectrum = jnp.dot(
        traces.reshape(windows_here * channels_here, length),
        dft_table(L, F, K0),
        preferred_element_type=jnp.float32,
    )
    energy = jnp.mean(spectrum * spectrum, axis=1, keepdims=True)
    scaled = (
        spectrum
        * lax.rsqrt(energy + 1e-06)
        * valid.reshape(windows_here * channels_here, 1).astype(jnp.float32)
    )
    white = jnp.transpose(
        scaled.astype(jnp.bfloat16).reshape(windows_here, channels_here, 2, F), (3, 2, 0, 1)
    )
    day_count = lax.axis_size("day")
    own_spectra = white.reshape(F, 2 * windows_here, channels_here)
    receiver_spectra = lax.all_gather(own_spectra, "row", axis=2, tiled=True)
    partial_terms = pair_maker(
        receiver_spectra, lax.all_gather(own_spectra, "col", axis=2, tiled=True)
    )
    summed = lax.psum_scatter(partial_terms, "day", scatter_dimension=1, tiled=True)
    stacked = summed * (1.0 / math.sqrt(windows_here * day_count))
    col_count = lax.axis_size("col")
    return stacked.reshape(2, stacked.shape[1], col_count, channels_here, stacked.shape[3])


def solution(mesh):
    placed = (P("day", ("col", "row"), None), P("day", ("col", "row")))
    return jax.shard_map(
        shards,
        mesh=mesh,
        in_specs=placed,
        out_specs=P(None, "day", None, "row", "col"),
        check_vma=False,
    )
```

profile of v0, /device:TPU:0, one launch (start us, length us, event | category | flops | bytes accessed | tf_op | source)
XLA Modules:
  0.0 128.7 jit_solution(10395836138942244168)
XLA Ops:
  6.5 0.0 copy-start
  6.5 0.0 copy-start.2
  6.5 0.0 all-reduce.3.cloned.1.call-start
  6.6 0.2 multiply_convert_fusion.2
  6.8 1.2 copy-done
  8.0 0.7 multiply_reduce_fusion
  8.7 0.0 copy-done.2
  8.8 0.1 copy.14
  8.9 0.1 convert_element_type.38
  8.9 0.1 fusion.4
  9.0 2.2 %reshape.51 = bf16[112,32,2,32]{1,0,3,2:T(8,128)(2,1)} reshape(bf16[3584,64]{0,1:T(8,128)(2,1)S(1)} %fusion.4) | data formatting | bytes 917504 | tf_op jit(solution)/shard_map/reshape | solution.py:53
  11.2 3.1 %copy.15 = bf16[32,2,112,32]{2,1,3,0:T(2,128)(2,1)S(1)} copy(bf16[32,2,112,32]{3,2,0,1:T(8,128)(2,1)} %bitcast.30) | data formatting | bytes 917504 | tf_op jit(solution)/shard_map/transpose | solution.py:52
  14.4 0.3 reshape.52
  14.7 15.6 %all_gather.6 = bf16[32,224,64]{1,2,0:T(8,128)(2,1)} all-gather(bf16[32,224,32]{1,2,0:T(8,128)(2,1)S(1)} %reshape.52), channel_id=1, replica_groups=mesh['day'=8,'row'=2,'col'=2] {'col'}, dimensions={2}, use_global_device_ids=true | all-gather | bytes 1376256 | tf_op jit(solution)/shard_map/all_gather | solution.py:59
  30.3 13.8 %all_gather.7 = bf16[32,224,64]{1,2,0:T(8,128)(2,1)S(1)} all-gather(bf16[32,224,32]{1,2,0:T(8,128)(2,1)S(1)} %reshape.52), channel_id=1, replica_groups=mesh['day'=8,'row'=2,'col'=2] {'row'}, dimensions={2}, use_global_device_ids=true | all-gather | bytes 1376256 | tf_op jit(solution)/shard_map/all_gather | solution.py:57
  44.1 2.4 %reshape.53 = bf16[32,2,112,64]{2,1,3,0:T(2,128)(2,1)} reshape(bf16[32,224,64]{1,2,0:T(8,128)(2,1)} %all_gather.6) | data formatting | bytes 1835008 | tf_op jit(solution)/shard_map/reshape | solution.py:28
  46.5 3.7 %fusion.18 = (bf16[32,1,112,64]{2,1,3,0:T(2,128)(2,1)S(1)}, bf16[32,1,112,64]{2,1,3,0:T(2,128)(2,1)S(1)}) fusion(bf16[32,2,112,64]{2,1,3,0:T(2,128)(2,1)} %reshape.53), kind=kLoop, calls=%fused_computation.34 | loop fusion | bytes 1835008 | tf_op jit(solution)/shard_map/slice | solution.py:29
  50.2 0.0 copy-start.1
  50.2 0.1 copy.26
  50.3 0.1 fusion.3
  50.4 1.0 copy-done.1
  51.4 0.4 convolution_bitcast_fusion.1
  51.8 0.5 convolution_bitcast_fusion
  52.4 1.5 %pad_maximum_fusion = f32[2,32,64,64]{3,2,1,0:T(8,128)} fusion(f32[1,32,64,64]{3,2,1,0:T(8,128)S(1)} %convolution_bitcast_fusion, f32[1,32,64,64]{3,2,1,0:T(8,128)S(1)} %convolution_bitcast_fusion.1), kind=kLoop, calls=%fused_computation | loop fusion | flops 262144 | bytes 2097152 | tf_op jit(solution)/shard_map/stack | solution.py:36
  53.8 0.0 copy-start.3
  53.8 0.0 all-reduce.3.cloned.1.call-update
  53.9 0.6 copy-done.3
  54.5 0.6 dynamic-slice
  55.7 64.4 %all-reduce.3.cloned.1.call-done = f32[2,32,64,64]{3,2,1,0:T(8,128)} async-done(((f32[2,32,64,64]{3,2,1,0:T(8,128)}), f32[2,32,64,64]{3,2,1,0:T(8,128)}) %all-reduce.3.cloned.1.call-update) | async-done | bytes 1048592
  120.2 1.7 %dynamic-slice_multiply_fusion = f32[2,4,64,64]{3,2,1,0:T(8,128)} fusion(f32[2,32,64,64]{3,2,1,0:T(8,128)} %all-reduce.3.cloned.1.call-done, u32[]{:T(128)S(6)} %multiply.7), kind=kLoop, calls=%fused_computation.12 | loop fusion | flops 32768 | bytes 262148 | tf_op jit(solution)/shard_map/mul | solution.py:62
  (4 shorter events, 0.1 us)
Async XLA Ops:
  6.5 1.5 %copy-start = (bf16[112,32,256]{2,1,0:T(8,128)(2,1)S(1)}, bf16[112,32,256]{2,1,0:T(8,128)(2,1)}, u32[]{:S(2)}) copy-start(bf16[112,32,256]{2,1,0:T(8,128)(2,1)} %param.2) | copy-start | bytes 5505028
  6.5 2.2 %copy-start.2 = (s32[112,32]{0,1:T(8,128)S(1)}, s32[112,32]{0,1:T(8,128)}, u32[]{:S(2)}) copy-start(s32[112,32]{0,1:T(8,128)} %param.3) | copy-start | bytes 43012
  6.5 113.6 %all-reduce.3.cloned.1.call-start = ((), (), s32[]{:S(2)}) async-start(), calls=%async_computation | async-start | bytes 4194304
  50.2 1.2 copy-start.1
  53.8 0.7 copy-start.3
Sparse Core Ops, SparseCore 0:
  54.0 66.1 all-reduce.2
where the time goes:
time: 129 us
  waiting for transfers between devices  64.5 us (50%)
  blocking collectives  29.4 us (23%)
  local copies, waits for them, and re-layouts  15.4 us (12%)
  between operations  14.2 us (11%)
  other arithmetic  3.62 us (3%)
  matrix products  1.62 us (1%)
    unnamed x2, waiting for transfers between devices  64.5 us
    all_gather x1, blocking collectives, shards(): lax.all_gather(own_spectra, 'col', axis=2, tiled=True)  15.6 us
    all_gather x1, blocking collectives, shards(): receiver_spectra = lax.all_gather(own_spectra, 'row', axis=2, tiled=True)  13.8 us
    slice x1, local copies, waits for them, and re-layouts, pair_maker(): turned = jnp.concatenate([halves[:, 1], -halves[:, 0]], axis=1)  3.66 us
    unnamed x10, local copies, waits for them, and re-layouts  3.53 us
    transpose x1, local copies, waits for them, and re-layouts, shards(): jnp.transpose(scaled.astype(jnp.bfloat16).reshape(windows_here, channels_...  3.15 us
  transfers between devices with their start and end apart: 1, of which 1 were waited for; matrix products, arithmetic and copies ran while one was open for 0% of the time, Pallas kernels for 0%

commit v1 on v0

--- a/solution.py
+++ b/solution.py
@@ -1,26 +1,257 @@
+import functools
 import math
 
 import jax
 import jax.numpy as jnp
+import numpy as np
 from jax import lax
+from jax.experimental import pallas as pl
+from jax.experimental.pallas import tpu as pltpu
 from jax.sharding import PartitionSpec as P
 
 L = 256
 F = 32
 K0 = 16
-
-
-def dft_table(length, nbins, first_bin):
-    sample = jnp.arange(length, dtype=jnp.int32)
-    bins = first_bin + jnp.arange(nbins, dtype=jnp.int32)
-    angle = (sample[:, None] * bins[None, :] % length).astype(jnp.float32) * (
+LANES = 128
+
+
+def dft_rows(length, bins):
+    sample = np.arange(length, dtype=np.int32)
+    bins = np.asarray(bins, dtype=np.int32)
+    angle = (sample[None, :] * bins[:, None] % length).astype(np.float32) * np.float32(
         2.0 * math.pi / length
     )
-    taper = 0.5 - 0.5 * jnp.cos((sample.astype(jnp.float32) + 0.5) * (2.0 * math.pi / length))
-    table = jnp.concatenate(
-        [taper[:, None] * jnp.cos(angle), -taper[:, None] * jnp.sin(angle)], axis=1
-    )
+    taper = np.float32(0.5) - np.float32(0.5) * np.cos(
+        (sample.astype(np.float32) + np.float32(0.5)) * np.float32(2.0 * math.pi / length)
+    )
+    table = np.concatenate([taper * np.cos(angle), -taper * np.sin(angle)], axis=0)
     return table.astype(jnp.bfloat16)
+
+
+def whiten_kernel(
+    traces_hbm, valid_hbm, table_hbm, white_ref, traces, valid, table, flags, pieces, sems
+):
+    chunks, span, channels, length = traces.shape
+    nbins = table.shape[0] // 2
+    windows = chunks * span
+    groups = chunks // 4
+    shard = 2 * lax.axis_index("col") + lax.axis_index("row")
+    late = lax.axis_index("day") // (lax.axis_size("day") // 2)
+
+    small = [
+        pltpu.make_async_copy(valid_hbm, valid, sems.at[groups]),
+        pltpu.make_async_copy(table_hbm.at[late], table, sems.at[groups + 1]),
+    ]
+    large = [
+        pltpu.make_async_copy(
+            traces_hbm.at[pl.ds(4 * g, 4)], traces.at[pl.ds(4 * g, 4)], sems.at[g]
+        )
+        for g in range(groups)
+    ]
+    for copy in small + large:
+        copy.start()
+    for copy in small:
+        copy.wait()
+
+    spread = jnp.concatenate([valid[...].astype(jnp.float32)] * span, axis=0)
+    place = lax.broadcasted_iota(jnp.int32, spread.shape, 0) // channels
+    window = lax.broadcasted_iota(jnp.int32, spread.shape, 1)
+    spread = jnp.where((window + shard) % span == place, spread, 0.0).astype(jnp.bfloat16)
+    pick = (
+        lax.broadcasted_iota(jnp.int32, (chunks, windows), 1) // span
+        == lax.broadcasted_iota(jnp.int32, (chunks, windows), 0)
+    )
+    flags[...] = lax.dot_general(
+        jnp.where(pick, 1.0, 0.0).astype(jnp.bfloat16),
+        spread,
+        (((1,), (1,)), ((), ())),
+        preferred_element_type=jnp.float32,
+    )
+
+    taps = table[...].astype(jnp.bfloat16)
+    turn = [lax.rem(w + span - shard, span) for w in range(span)]
+    for group in range(groups):
+        if group % 3 == 0:
+            for copy in large[group : group + 3]:
+                copy.wait()
+        samples = [traces[4 * group + c, turn[w]] for c in range(4) for w in range(span)]
+        spectrum = lax.dot_general(
+            taps,
+            jnp.concatenate(samples, axis=0),
+            (((1,), (1,)), ((), ())),
+            preferred_element_type=jnp.float32,
+        )
+        energy = jnp.sum(spectrum * spectrum, axis=0, keepdims=True) * (1.0 / (2 * nbins))
+        gain = lax.rsqrt(energy + 1e-06)
+        for part in range(4):
+            lanes = slice(part * LANES, (part + 1) * LANES)
+            scaled = spectrum[:, lanes] * (
+                gain[:, lanes] * flags[pl.ds(4 * group + part, 1), :]
+            )
+            pieces[group, pl.ds(part, nbins, stride=8), :] = scaled[:nbins]
+            pieces[group, pl.ds(4 + part, nbins, stride=8), :] = scaled[nbins:]
+        done = pieces[group].astype(white_ref.dtype)
+        white_ref[:, group] = done.reshape(nbins // 2, 16, LANES)
+
+
+def spreading(shape):
+    row = lax.broadcasted_iota(jnp.int32, shape, 0).astype(jnp.float32)
+    lane = lax.broadcasted_iota(jnp.int32, shape, 1).astype(jnp.float32)
+    turn = row * 0.618034 + lane * 0.7548777
+    return turn - jnp.floor(turn)
+
+
+def in_first_group():
+    day, half = lax.axis_index("day"), lax.axis_size("day") // 2
+    return jnp.where((day % half) ^ (day // half) == 0, 1, 0)
+
+
+def cross_kernel(channels, factor, pieces_ref, blocks_ref):
+    shards = LANES // channels
+    rows = pieces_ref.shape[0] // (shards * 2)
+    half = LANES // 2
+    turned_round = in_first_group()
+    pieces = pieces_ref[...].astype(jnp.float32).reshape(shards, rows // 8, 2, 8, LANES)
+    lane = lax.broadcasted_iota(jnp.int32, (rows, LANES), 1) // channels
+    low = lax.broadcasted_iota(jnp.int32, (channels, LANES), 1) < half
+    scale = jnp.exp2(spreading((2 * channels, LANES))) * factor
+
+    for h in range(2):
+        parts = [pieces[shards - 1 - s, :, h].reshape(rows, LANES) for s in range(shards)]
+        merged = []
+        for w in range(shards):
+            row_of = parts[-w % shards]
+            for g in range(1, shards):
+                row_of = jnp.where(lane == g, parts[(g - w) % shards], row_of)
+            merged.append(pltpu.roll(row_of, LANES - w * channels, 1) if w else row_of)
+        spectra = jnp.concatenate(merged, axis=0)
+        turned = pltpu.roll(spectra.reshape(-1, 8, LANES), 4, 1).reshape(spectra.shape)
+        place = lax.broadcasted_iota(jnp.int32, spectra.shape, 0)
+        turned = jnp.where(place % 8 < 4, turned, -turned)
+        cross = lax.dot_general(
+            jnp.concatenate([spectra, turned], axis=1).astype(jnp.bfloat16),
+            spectra.astype(jnp.bfloat16),
+            (((0,), (0,)), ((), ())),
+            preferred_element_type=jnp.float32,
+        )
+        for q in range(4):
+            col, row = q // 2, q % 2
+            both = []
+            for b in range(2):
+                first = (2 * b + row) * channels
+                real = cross[first : first + channels]
+                imag = cross[LANES + first : LANES + first + channels]
+                if col == 0:
+                    both.append(jnp.where(low, real, pltpu.roll(imag, half, 1)))
+                else:
+                    both.append(jnp.where(low, pltpu.roll(real, half, 1), imag))
+            block = jnp.concatenate(both, axis=0) * scale
+            first = pl.multiple_of((4 * h + (q ^ (3 * turned_round))) * 2 * channels, 2 * channels)
+            blocks_ref[pl.ds(first, 2 * channels), :] = block.astype(blocks_ref.dtype)
+
+
+def place_kernel(blocks_ref, out_hbm, out, sems):
+    _, bins, _, channels, half = out.shape
+    height = 2 * channels
+    turned_round = in_first_group()
+    scale = jnp.exp2(-spreading((height, 2 * half)))
+    copies = [
+        pltpu.make_async_copy(out.at[:, q], out_hbm.at[:, q], sems.at[q]) for q in range(bins)
+    ]
+    for q in range(bins):
+        at = [pl.multiple_of((4 * h + (q ^ (3 * turned_round))) * height, height) for h in range(2)]
+        pair = [blocks_ref[pl.ds(first, height), :].astype(jnp.float32) for first in at]
+        block = (pair[0] + pair[1]) * scale
+        for b in range(2):
+            out[0, q, b, :, :] = block[b * channels : (b + 1) * channels, :half]
+            out[1, q, b, :, :] = block[b * channels : (b + 1) * channels, half:]
+        copies[q].start()
+    for copy in copies:
+        copy.wait()
+
+
+def two_bins_each(traces, valid):
+    windows, channels, length = traces.shape
+    days = lax.axis_size("day")
+    half = days // 2
+    span = LANES // channels
+    chunks = windows // span
+    groups = chunks // 4
+    members = [
+        (q, 2 * chip + core)
+        for q in (3, 2, 1, 0)
+        for core in (1, 0)
+        for chip in range(half // 2)[::-1]
+    ]
+    in_half = [[4 * (h * half + day) + q for q, day in members] for h in range(2)]
+
+    def halves(day):
+        return (1, 0) if day // 2 % 2 == 0 else (0, 1)
+
+    def places(day):
+        return (3, 2, 1, 0) if day == 0 else (0, 1, 2, 3)
+
+    over_halves = [
+        [4 * (h * half + (day ^ h)) + q for h in halves(day) for q in places(day)]
+        for day in range(half)
+    ]
+    tables = [
+        [K0 + 4 * (h * half + (day ^ h ^ late)) + q for q, day in members for h in halves(day)]
+        for late in range(2)
+    ]
+
+    vmem = pl.BlockSpec(memory_space=pltpu.VMEM)
+    hbm = pl.BlockSpec(memory_space=pltpu.HBM)
+    params = pltpu.CompilerParams(vmem_limit_bytes=32 * 1024 * 1024)
+    white = pl.pallas_call(
+        whiten_kernel,
+        out_shape=jax.ShapeDtypeStruct((F // 2, groups, 16, LANES), jnp.bfloat16),
+        in_specs=[hbm] * 3,
+        out_specs=vmem,
+        scratch_shapes=[
+            pltpu.VMEM((chunks, span, channels, length), jnp.bfloat16),
+            pltpu.VMEM((channels, windows), jnp.int32),
+            pltpu.VMEM((2 * F, length), jnp.float32),
+            pltpu.VMEM((chunks, LANES), jnp.float32),
+            pltpu.VMEM((groups, 8 * F, LANES), jnp.float32),
+            pltpu.SemaphoreType.DMA((groups + 2,)),
+        ],
+        compiler_params=params,
+        name="whiten",
+    )(
+        *(
+            pltpu.with_memory_space_constraint(operand, pltpu.HBM)
+            for operand in (
+                traces.reshape(chunks, span, channels, length),
+                valid.T,
+                np.stack([dft_rows(L, bins).astype(np.float32) for bins in tables]),
+            )
+        )
+    )
+    everyone = ("day", "col", "row")
+    white = white.reshape(-1, LANES)
+    pieces = lax.all_to_all(white, everyone, 0, 0, axis_index_groups=in_half, tiled=True)
+    blocks = pl.pallas_call(
+        functools.partial(cross_kernel, channels, 1.0 / math.sqrt(windows * days)),
+        out_shape=jax.ShapeDtypeStruct((8 * 2 * channels, LANES), jnp.bfloat16),
+        in_specs=[vmem],
+        out_specs=vmem,
+        compiler_params=params,
+        name="cross",
+    )(pieces)
+    placed = lax.all_to_all(blocks, everyone, 0, 0, axis_index_groups=over_halves, tiled=True)
+    return pl.pallas_call(
+        place_kernel,
+        out_shape=jax.ShapeDtypeStruct((2, 4, 2, channels, LANES // 2), jnp.float32),
+        in_specs=[vmem],
+        out_specs=hbm,
+        scratch_shapes=[
+            pltpu.VMEM((2, 4, 2, channels, LANES // 2), jnp.float32),
+            pltpu.SemaphoreType.DMA((4,)),
+        ],
+        compiler_params=params,
+        name="place",
+    )(placed)
 
 
 def pair_maker(receiver_spectra, source_part):
@@ -36,11 +267,11 @@
     return jnp.stack([real_part, imag_part])
 
 
-def shards(traces, valid):
+def gathered(traces, valid):
     windows_here, channels_here, length = traces.shape
     spectrum = jnp.dot(
         traces.reshape(windows_here * channels_here, length),
-        dft_table(L, F, K0),
+        jnp.asarray(dft_rows(L, range(K0, K0 + F)).T),
         preferred_element_type=jnp.float32,
     )
     energy = jnp.mean(spectrum * spectrum, axis=1, keepdims=True)
@@ -62,6 +293,20 @@
     stacked = summed * (1.0 / math.sqrt(windows_here * day_count))
     col_count = lax.axis_size("col")
     return stacked.reshape(2, stacked.shape[1], col_count, channels_here, stacked.shape[3])
+
+
+def shards(traces, valid):
+    windows, channels, _ = traces.shape
+    cols, rows = lax.axis_size("col"), lax.axis_size("row")
+    owners = lax.axis_size("day") * cols * rows
+    fits = (
+        owners == F
+        and cols == 2
+        and rows == 2
+        and cols * rows * channels == LANES
+        and windows * channels % (4 * LANES) == 0
+    )
+    return two_bins_each(traces, valid) if fits else gathered(traces, valid)
 
 
 def solution(mesh):

time: 129 us -> 27.2 us (0.21)
  the two profiles are of different devices: /device:TPU:0 before, /device:TPU:9 now
where the time goes in v1:
time: 27.2 us; the launch traced here: 27 us
  blocking collectives  23 us (85%)
  Pallas kernels  3.91 us (14%)
    all_to_all x1, blocking collectives, two_bins_each(): lax.all_to_all(white, everyone, 0, 0, axis_index_groups=in_half, tiled=True)  11.7 us
    all_to_all x1, blocking collectives, two_bins_each(): lax.all_to_all(blocks, everyone, 0, 0, axis_index_groups=over_halves, til...  11.4 us
    pallas_call x1, Pallas kernels, two_bins_each(): pl.pallas_call(whiten_kernel, out_shape=jax.ShapeDtypeStruct((F // 2, gro...  2.32 us
    pallas_call x1, Pallas kernels, two_bins_each(): pl.pallas_call(place_kernel, out_shape=jax.ShapeDtypeStruct((2, 4, 2, cha...  0.82 us
    pallas_call x1, Pallas kernels, two_bins_each(): pl.pallas_call(functools.partial(cross_kernel, channels, 1.0 / math.sqrt(...  0.77 us

profile of v1, /device:TPU:9, one launch (start us, length us, event | category | flops | bytes accessed | tf_op | source)
XLA Modules:
  0.0 27.0 jit_solution(11209798148536662977)
XLA Ops:
  0.0 2.3 %whiten.1 = bf16[16,7,16,128]{3,2,1,0:T(8,128)(2,1)S(1)} custom-call(bf16[28,4,32,256]{3,2,1,0:T(8,128)(2,1)} %bitcast.10, s32[32,112]{1,0:T(8,128)} %bitcast.11, f32[2,64,256]{2,1,0:T(8,128)} %constant.2.clone.table_hbm), custom_call_target="tpu_custom_call" | custom-call | tf_op jit(solution)/shard_map/whiten/pallas_call | solution.py:206
  2.3 11.7 %all_to_all.22 = bf16[16,112,128]{2,1,0:T(8,128)(2,1)S(1)} all-to-all(bf16[16,112,128]{2,1,0:T(8,128)(2,1)S(1)} %bitcast.6), channel_id=1, replica_groups={{15,7,11,3,13,5,9,1,14,6,10,2,12,4,8,0},{31,23,27,19,29,21,25,17,30,22,..., dimensions={0} | all-to-all | bytes 917504 | tf_op jit(solution)/shard_map/all_to_all | solution.py:233
  14.0 0.8 %cross.1 = bf16[512,128]{1,0:T(8,128)(2,1)S(1)} custom-call(bf16[1792,128]{1,0:T(8,128)(2,1)S(1)} %bitcast.7), custom_call_target="tpu_custom_call" | custom-call | tf_op jit(solution)/shard_map/cross/pallas_call | solution.py:234
  14.8 11.4 %all_to_all.23 = bf16[8,64,128]{2,1,0:T(8,128)(2,1)S(1)} all-to-all(bf16[8,64,128]{2,1,0:T(8,128)(2,1)S(1)} %bitcast.9), channel_id=1, replica_groups={{23,21,22,20,3,1,2,0},{16,18,17,19,4,6,5,7},{8,10,9,11,28,30,29,31},{12..., dimensions={0} | all-to-all | bytes 262144 | tf_op jit(solution)/shard_map/all_to_all | solution.py:242
  26.1 0.8 %place.1 = f32[2,4,2,32,64]{4,3,2,1,0:T(8,128)} custom-call(bf16[512,128]{1,0:T(8,128)(2,1)S(1)} %bitcast.8), custom_call_target="tpu_custom_call" | custom-call | tf_op jit(solution)/shard_map/place/pallas_call | solution.py:243

commit v2 on v1

--- a/solution.py
+++ b/solution.py
@@ -101,16 +101,10 @@
     return turn - jnp.floor(turn)
 
 
-def in_first_group():
-    day, half = lax.axis_index("day"), lax.axis_size("day") // 2
-    return jnp.where((day % half) ^ (day // half) == 0, 1, 0)
-
-
 def cross_kernel(channels, factor, pieces_ref, blocks_ref):
     shards = LANES // channels
     rows = pieces_ref.shape[0] // (shards * 2)
     half = LANES // 2
-    turned_round = in_first_group()
     pieces = pieces_ref[...].astype(jnp.float32).reshape(shards, rows // 8, 2, 8, LANES)
     lane = lax.broadcasted_iota(jnp.int32, (rows, LANES), 1) // channels
     low = lax.broadcasted_iota(jnp.int32, (channels, LANES), 1) < half
@@ -146,21 +140,22 @@
                 else:
                     both.append(jnp.where(low, pltpu.roll(real, half, 1), imag))
             block = jnp.concatenate(both, axis=0) * scale
-            first = pl.multiple_of((4 * h + (q ^ (3 * turned_round))) * 2 * channels, 2 * channels)
+            first = (4 * h + 3 - q) * 2 * channels
             blocks_ref[pl.ds(first, 2 * channels), :] = block.astype(blocks_ref.dtype)
 
 
 def place_kernel(blocks_ref, out_hbm, out, sems):
     _, bins, _, channels, half = out.shape
     height = 2 * channels
-    turned_round = in_first_group()
     scale = jnp.exp2(-spreading((height, 2 * half)))
     copies = [
         pltpu.make_async_copy(out.at[:, q], out_hbm.at[:, q], sems.at[q]) for q in range(bins)
     ]
     for q in range(bins):
-        at = [pl.multiple_of((4 * h + (q ^ (3 * turned_round))) * height, height) for h in range(2)]
-        pair = [blocks_ref[pl.ds(first, height), :].astype(jnp.float32) for first in at]
+        pair = [
+            blocks_ref[pl.ds((4 * h + 3 - q) * height, height), :].astype(jnp.float32)
+            for h in range(2)
+        ]
         block = (pair[0] + pair[1]) * scale
         for b in range(2):
             out[0, q, b, :, :] = block[b * channels : (b + 1) * channels, :half]
@@ -177,23 +172,15 @@
     span = LANES // channels
     chunks = windows // span
     groups = chunks // 4
-    members = [
-        (q, 2 * chip + core)
-        for q in (3, 2, 1, 0)
-        for core in (1, 0)
-        for chip in range(half // 2)[::-1]
-    ]
+    chips = [day for core in range(2) for day in range(core, half, 2)]
+    members = [(q, day) for q in (3, 2, 1, 0) for day in range(half)[::-1]]
     in_half = [[4 * (h * half + day) + q for q, day in members] for h in range(2)]
 
     def halves(day):
         return (1, 0) if day // 2 % 2 == 0 else (0, 1)
 
-    def places(day):
-        return (3, 2, 1, 0) if day == 0 else (0, 1, 2, 3)
-
     over_halves = [
-        [4 * (h * half + (day ^ h)) + q for h in halves(day) for q in places(day)]
-        for day in range(half)
+        [4 * (h * half + (day ^ h)) + q for h in halves(day) for q in (3, 2, 1, 0)] for day in chips
     ]
     tables = [
         [K0 + 4 * (h * half + (day ^ h ^ late)) + q for q, day in members for h in halves(day)]

time: 27.2 us -> 26.8 us (0.985)
  the two profiles are of different devices: /device:TPU:9 before, /device:TPU:0 now
where the time goes in v2:
time: 26.8 us; the launch traced here: 26.5 us
  blocking collectives  22.6 us (84%)
  Pallas kernels  3.91 us (15%)
    all_to_all x1, blocking collectives, two_bins_each(): lax.all_to_all(white, everyone, 0, 0, axis_index_groups=in_half, tiled=True)  13.5 us
    all_to_all x1, blocking collectives, two_bins_each(): lax.all_to_all(blocks, everyone, 0, 0, axis_index_groups=over_halves, til...  9.05 us
    pallas_call x1, Pallas kernels, two_bins_each(): pl.pallas_call(whiten_kernel, out_shape=jax.ShapeDtypeStruct((F // 2, gro...  2.32 us
    pallas_call x1, Pallas kernels, two_bins_each(): pl.pallas_call(place_kernel, out_shape=jax.ShapeDtypeStruct((2, 4, 2, cha...  0.82 us
    pallas_call x1, Pallas kernels, two_bins_each(): pl.pallas_call(functools.partial(cross_kernel, channels, 1.0 / math.sqrt(...  0.77 us

profile of v2, /device:TPU:0, one launch (start us, length us, event | category | flops | bytes accessed | tf_op | source)
XLA Modules:
  0.0 26.5 jit_solution(7405430329090822470)
XLA Ops:
  0.0 2.3 %whiten.1 = bf16[16,7,16,128]{3,2,1,0:T(8,128)(2,1)S(1)} custom-call(bf16[28,4,32,256]{3,2,1,0:T(8,128)(2,1)} %bitcast.10, s32[32,112]{1,0:T(8,128)} %bitcast.11, f32[2,64,256]{2,1,0:T(8,128)} %constant.2.clone.table_hbm), custom_call_target="tpu_custom_call" | custom-call | tf_op jit(solution)/shard_map/whiten/pallas_call | solution.py:193
  2.3 13.5 %all_to_all.22 = bf16[16,112,128]{2,1,0:T(8,128)(2,1)S(1)} all-to-all(bf16[16,112,128]{2,1,0:T(8,128)(2,1)S(1)} %bitcast.6), channel_id=1, replica_groups={{15,11,7,3,13,9,5,1,14,10,6,2,12,8,4,0},{31,27,23,19,29,25,21,17,30,26,..., dimensions={0} | all-to-all | bytes 917504 | tf_op jit(solution)/shard_map/all_to_all | solution.py:220
  15.8 0.8 %cross.1 = bf16[512,128]{1,0:T(8,128)(2,1)S(1)} custom-call(bf16[1792,128]{1,0:T(8,128)(2,1)S(1)} %bitcast.7), custom_call_target="tpu_custom_call" | custom-call | tf_op jit(solution)/shard_map/cross/pallas_call | solution.py:221
  16.6 9.1 %all_to_all.23 = bf16[8,64,128]{2,1,0:T(8,128)(2,1)S(1)} all-to-all(bf16[8,64,128]{2,1,0:T(8,128)(2,1)S(1)} %bitcast.9), channel_id=1, replica_groups={{23,21,22,20,3,1,2,0},{11,9,10,8,31,29,30,28},{19,17,18,16,7,5,6,4},{15..., dimensions={0} | all-to-all | bytes 262144 | tf_op jit(solution)/shard_map/all_to_all | solution.py:229
  25.7 0.8 %place.1 = f32[2,4,2,32,64]{4,3,2,1,0:T(8,128)} custom-call(bf16[512,128]{1,0:T(8,128)(2,1)S(1)} %bitcast.8), custom_call_target="tpu_custom_call" | custom-call | tf_op jit(solution)/shard_map/place/pallas_call | solution.py:230

commit v3 on v2

--- a/solution.py
+++ b/solution.py
@@ -50,7 +50,7 @@
     ]
     for copy in small + large:
         copy.start()
-    for copy in small:
+    for copy in small + large[:3]:
         copy.wait()
 
     spread = jnp.concatenate([valid[...].astype(jnp.float32)] * span, axis=0)
@@ -71,7 +71,7 @@
     taps = table[...].astype(jnp.bfloat16)
     turn = [lax.rem(w + span - shard, span) for w in range(span)]
     for group in range(groups):
-        if group % 3 == 0:
+        if group and group % 3 == 0:
             for copy in large[group : group + 3]:
                 copy.wait()
         samples = [traces[4 * group + c, turn[w]] for c in range(4) for w in range(span)]
@@ -90,7 +90,7 @@
             )
             pieces[group, pl.ds(part, nbins, stride=8), :] = scaled[:nbins]
             pieces[group, pl.ds(4 + part, nbins, stride=8), :] = scaled[nbins:]
-        done = pieces[group].astype(white_ref.dtype)
+        done = pieces[group, pl.ds(0, 8 * nbins), :].astype(white_ref.dtype)
         white_ref[:, group] = done.reshape(nbins // 2, 16, LANES)
 
 
@@ -200,7 +200,7 @@
             pltpu.VMEM((channels, windows), jnp.int32),
             pltpu.VMEM((2 * F, length), jnp.float32),
             pltpu.VMEM((chunks, LANES), jnp.float32),
-            pltpu.VMEM((groups, 8 * F, LANES), jnp.float32),
+            pltpu.VMEM((groups, 8 * F + 8, LANES), jnp.float32),
             pltpu.SemaphoreType.DMA((groups + 2,)),
         ],
         compiler_params=params,

time: 26.8 us -> 26.8 us (level)
  no operation moved by 1% of the time
where the time goes in v3:
time: 26.8 us; the launch traced here: 26.5 us
  blocking collectives  22.6 us (84%)
  Pallas kernels  3.92 us (15%)
    all_to_all x1, blocking collectives, two_bins_each(): lax.all_to_all(white, everyone, 0, 0, axis_index_groups=in_half, tiled=True)  13.5 us
    all_to_all x1, blocking collectives, two_bins_each(): lax.all_to_all(blocks, everyone, 0, 0, axis_index_groups=over_halves, til...  9.06 us
    pallas_call x1, Pallas kernels, two_bins_each(): pl.pallas_call(whiten_kernel, out_shape=jax.ShapeDtypeStruct((F // 2, gro...  2.33 us
    pallas_call x1, Pallas kernels, two_bins_each(): pl.pallas_call(place_kernel, out_shape=jax.ShapeDtypeStruct((2, 4, 2, cha...  0.82 us
    pallas_call x1, Pallas kernels, two_bins_each(): pl.pallas_call(functools.partial(cross_kernel, channels, 1.0 / math.sqrt(...  0.77 us

profile of v3, /device:TPU:0, one launch (start us, length us, event | category | flops | bytes accessed | tf_op | source)
XLA Modules:
  0.0 26.5 jit_solution(7626131474446894912)
XLA Ops:
  0.0 2.3 %whiten.1 = bf16[16,7,16,128]{3,2,1,0:T(8,128)(2,1)S(1)} custom-call(bf16[28,4,32,256]{3,2,1,0:T(8,128)(2,1)} %bitcast.10, s32[32,112]{1,0:T(8,128)} %bitcast.11, f32[2,64,256]{2,1,0:T(8,128)} %constant.2.clone.table_hbm), custom_call_target="tpu_custom_call" | custom-call | tf_op jit(solution)/shard_map/whiten/pallas_call | solution.py:193
  2.3 13.5 %all_to_all.22 = bf16[16,112,128]{2,1,0:T(8,128)(2,1)S(1)} all-to-all(bf16[16,112,128]{2,1,0:T(8,128)(2,1)S(1)} %bitcast.6), channel_id=1, replica_groups={{15,11,7,3,13,9,5,1,14,10,6,2,12,8,4,0},{31,27,23,19,29,25,21,17,30,26,..., dimensions={0} | all-to-all | bytes 917504 | tf_op jit(solution)/shard_map/all_to_all | solution.py:220
  15.8 0.8 %cross.1 = bf16[512,128]{1,0:T(8,128)(2,1)S(1)} custom-call(bf16[1792,128]{1,0:T(8,128)(2,1)S(1)} %bitcast.7), custom_call_target="tpu_custom_call" | custom-call | tf_op jit(solution)/shard_map/cross/pallas_call | solution.py:221
  16.6 9.1 %all_to_all.23 = bf16[8,64,128]{2,1,0:T(8,128)(2,1)S(1)} all-to-all(bf16[8,64,128]{2,1,0:T(8,128)(2,1)S(1)} %bitcast.9), channel_id=1, replica_groups={{23,21,22,20,3,1,2,0},{11,9,10,8,31,29,30,28},{19,17,18,16,7,5,6,4},{15..., dimensions={0} | all-to-all | bytes 262144 | tf_op jit(solution)/shard_map/all_to_all | solution.py:229
  25.7 0.8 %place.1 = f32[2,4,2,32,64]{4,3,2,1,0:T(8,128)} custom-call(bf16[512,128]{1,0:T(8,128)(2,1)S(1)} %bitcast.8), custom_call_target="tpu_custom_call" | custom-call | tf_op jit(solution)/shard_map/place/pallas_call | solution.py:230
